TPU v7x, 32 devices: a whole 2x2x4 slice. The times are simulated.
32 devices in a mesh: section: 8 (over z, x), dp: 4 (over y, core).
Axes of the slice: x: 2, y: 2, z: 4, core: 2. Of those that a mesh axis runs over, the one named last changes fastest.
Arguments:
- activations: bfloat16 [8, 16, 64, 8192], P('section', 'dp'), may hold values from -6 to 6
- out_grads: bfloat16 [8, 16, 64, 8192], P('section', 'dp'), may hold values from -6 to 6
- proj_in: bfloat16 [8, 64, 8192], P('section'), may hold values from -0.0625 to 0.0625
- proj_out: bfloat16 [8, 64, 8192], P('section'), may hold values from -0.0625 to 0.0625
- queries: bfloat16 [8, 64, 4096], P('section', 'dp'), may hold values from -6 to 6
- lengths: int32 [4, 4], P('dp'), may hold values from 1 to 64, 160 in all within a row
Outputs:
- scores: float32 [16, 64], P('dp')
Inputs may be any that keep to these rules, and one draw needn't show every extreme that they name: `lengths`: the 4 examples of each data group use 5 * 32 tokens together, and one of them all 64.
All inputs are finite; a program needn't handle non-finite values.
Results may differ from a plain program's by a relative error of at most 0.005.
Values may be sent and summed in bfloat16 or wider, within the bound.
A program may use at most 64 MiB of HBM per device.

v0:
```python
import jax
import jax.numpy as jnp
from jax import lax
from jax.sharding import PartitionSpec as P


def body(activations, out_grads, proj_in, proj_out, queries, lengths):
    layer_acts = activations[0]
    layer_grads = out_grads[0]
    examples_here = layer_acts.shape[0]
    seq_slots = layer_acts.shape[1]
    width = layer_acts.shape[2]
    rank = proj_in.shape[1]
    lengths_flat = lengths.reshape(-1)
    positions = jnp.arange(seq_slots, dtype=jnp.int32)
    token_mask = (positions[None, :] < lengths_flat[:, None]).astype(jnp.bfloat16)
    in_coords = jnp.dot(
        layer_acts.reshape(-1, width), proj_in[0].T, preferred_element_type=jnp.float32
    )
    in_coords = (
        in_coords.astype(jnp.bfloat16).reshape(examples_here, seq_slots, rank)
        * token_mask[:, :, None]
    )
    out_coords = jnp.dot(
        layer_grads.reshape(-1, width), proj_out[0].T, preferred_element_type=jnp.float32
    )
    out_coords = out_coords.astype(jnp.bfloat16).reshape(examples_here, seq_slots, rank)
    projected = jnp.einsum(
        "esj,esk->ejk", out_coords, in_coords, preferred_element_type=jnp.float32
    )
    projected = projected.astype(jnp.bfloat16).reshape(examples_here, rank * rank)
    norm_factor = 1.0 / (rank * (seq_slots * lax.axis_size("section")) ** 0.5)
    all_grads = lax.all_gather(projected, "dp", axis=0, tiled=True)
    partial_scores = jnp.dot(all_grads, queries[0].T, preferred_element_type=jnp.float32)
    layer_scores = lax.psum(partial_scores, "section")
    summed_scores = lax.all_to_all(layer_scores, "dp", split_axis=0, concat_axis=1, tiled=True)
    return summed_scores * norm_factor


def solution(mesh):
    placed = (
        P("section", "dp", None, None),
        P("section", "dp", None, None),
        P("section", None, None),
        P("section", None, None),
        P("section", "dp", None),
        P("dp", None),
    )
    return jax.shard_map(body, mesh=mesh, in_specs=placed, out_specs=P("dp", None), check_vma=False)
```

profile of v0, /device:TPU:0, one launch (start us, length us, event | category | flops | bytes accessed | tf_op | source)
XLA Modules:
  0.0 45.1 jit_solution(16739431354762134637)
XLA Ops:
  0.0 0.0 copy-start
  0.0 0.0 copy-start.1
  0.0 0.9 %fusion.7 = bf16[4,64]{1,0:T(4,128)(2,1)S(1)} fusion(s32[4]{0:T(128)} %bitcast.25), kind=kLoop, calls=%fused_computation.12 | loop fusion | flops 512 | bytes 528 | tf_op jit(solution)/shard_map/convert_element_type | solution.py:16
  0.9 0.4 copy-done
  1.2 3.6 %convolution_convert_fusion.1 = bf16[256,64]{0,1:T(8,128)(2,1)S(1)} fusion(bf16[256,8192]{1,0:T(8,128)(2,1)} %bitcast.21, bf16[1,64,8192]{2,1,0:T(8,128)(2,1)S(1)} %copy-done), kind=kOutput, calls=%fused_computation.1 | convolution fusion | flops 268451840 | bytes 5275648 | tf_op jit(solution)/shard_map/dot_general | solution.py:17
  4.8 0.0 copy-start.2
  4.8 0.1 copy.13
  4.9 0.0 copy-done.1
  5.0 3.6 %convolution_convert_fusion.2 = bf16[256,64]{0,1:T(8,128)(2,1)S(1)} fusion(bf16[256,8192]{1,0:T(8,128)(2,1)} %bitcast.22, bf16[1,64,8192]{2,1,0:T(8,128)(2,1)S(1)} %copy-done.1), kind=kOutput, calls=%fused_computation.2 | convolution fusion | flops 268451840 | bytes 5275648 | tf_op jit(solution)/shard_map/dot_general | solution.py:24
  8.5 0.1 reshape.39
  8.7 0.2 convolution_convert_fusion
  8.9 0.1 reshape.42
  9.0 6.5 %all-gather = bf16[4,4,4096]{2,1,0:T(4,128)(2,1)S(1)} all-gather(bf16[1,4,4096]{2,1,0:T(4,128)(2,1)S(1)} %reshape.42), channel_id=1, replica_groups=mesh['section'=8,'dp'=4] {'dp'}, dimensions={0}, use_global_device_ids=true | all-gather | bytes 163840 | tf_op jit(solution)/shard_map/all_gather | solution.py:33
  15.6 0.0 copy-done.2
  15.6 0.2 fusion.2
  15.7 22.3 %psum.7 = f32[4,4,16]{2,1,0:T(4,128)S(1)} all-reduce(f32[4,4,16]{2,1,0:T(4,128)S(1)} %bitcast.24), channel_id=1, replica_groups=mesh['section'=8,'dp'=4] {'section'}, use_global_device_ids=true, to_apply=%region_0.0 | all-reduce | flops 256 | bytes 2048 | tf_op jit(solution)/shard_map/psum | solution.py:35
  38.0 6.4 %all_to_all.13 = f32[4,4,16]{2,1,0:T(4,128)S(1)} all-to-all(f32[4,4,16]{2,1,0:T(4,128)S(1)} %psum.7), channel_id=1, replica_groups=mesh['section'=8,'dp'=4] {'dp'}, dimensions={0} | all-to-all | bytes 2048 | tf_op jit(solution)/shard_map/all_to_all | solution.py:36
  44.4 0.7 %mul.25 = f32[4,64]{1,0:T(4,128)} reshape(f32[4,4,16]{2,1,0:T(4,128)S(1)} %copy.12) | data formatting | bytes 2048 | tf_op jit(solution)/shard_map/mul | solution.py:37
  (3 shorter events, 0.0 us)
Async XLA Ops:
  0.0 1.2 %copy-start = (bf16[1,64,8192]{2,1,0:T(8,128)(2,1)S(1)}, bf16[1,64,8192]{2,1,0:T(8,128)(2,1)}, u32[]{:S(2)}) copy-start(bf16[1,64,8192]{2,1,0:T(8,128)(2,1)} %param.8) | copy-start | bytes 3145732
  0.0 4.9 %copy-start.1 = (bf16[1,64,8192]{2,1,0:T(8,128)(2,1)S(1)}, bf16[1,64,8192]{2,1,0:T(8,128)(2,1)}, u32[]{:S(2)}) copy-start(bf16[1,64,8192]{2,1,0:T(8,128)(2,1)} %param.9) | copy-start | bytes 3145732
  4.8 10.7 %copy-start.2 = (bf16[1,16,4096]{2,1,0:T(8,128)(2,1)S(1)}, bf16[1,16,4096]{2,1,0:T(8,128)(2,1)}, u32[]{:S(2)}) copy-start(bf16[1,16,4096]{2,1,0:T(8,128)(2,1)} %param.10) | copy-start | bytes 393220
where the time goes:
time: 45.3 us; the launch traced here: 45.1 us
  blocking collectives  35.2 us (78%)
  matrix products  7.55 us (17%)
  local copies, waits for them, and re-layouts  1.41 us (3%)
  other arithmetic  0.88 us (2%)
    psum x1, blocking collectives, body(): layer_scores = lax.psum(partial_scores, 'section')  22.3 us
    all_gather x1, blocking collectives, body(): all_grads = lax.all_gather(projected, 'dp', axis=0, tiled=True)  6.51 us
    all_to_all x1, blocking collectives, body(): lax.all_to_all(layer_scores, 'dp', split_axis=0, concat_axis=1, tiled=True)  6.4 us
    dot_general x1, matrix products, body(): jnp.dot(layer_grads.reshape(-1, width), proj_out[0].T, preferred_element_...  3.58 us
    dot_general x1, matrix products, body(): jnp.dot(layer_acts.reshape(-1, width), proj_in[0].T, preferred_element_ty...  3.58 us

commit v1 on v0

v1 whole, which is shorter than its diff:
```python
import functools

import jax
import jax.numpy as jnp
from jax import lax
from jax.experimental import pallas as pl
from jax.experimental.pallas import tpu as pltpu
from jax.sharding import PartitionSpec as P

MESH = pl.DeviceIdType.MESH
CHUNKS = 8
PIECES = 2
NT = (((1,), (1,)), ((), ()))


def kernel(
    n_sec, n_dp, n_ex,
    acts, grads, p_in, p_out, queries, lengths, out,
    a_v, g_v, pi_v, po_v, q_v, len_s, rows_v, part_v, recv_v,
    load_sem, own_sem, len_sem, far_send, far_recv, fwd_send, fwd_recv,
    sib_send, sib_recv, sum_send, sum_recv,
):
    me_s, me_d = lax.axis_index("section"), lax.axis_index("dp")
    n_chips = n_dp // 2
    chip, core = me_d // 2, lax.rem(me_d, 2)
    sibling = chip * 2 + 1 - core

    def chip_at(step):
        return lax.rem(chip + step + n_chips, n_chips) * 2 + core

    def section_at(step):
        return lax.rem(me_s + step + n_sec, n_sec)

    rows, width = acts.shape
    rank = p_in.shape[0]
    slots = rows // n_ex
    depth = queries.shape[1]
    cols = width // CHUNKS
    piece = depth // PIECES

    barrier = pltpu.get_barrier_semaphore()
    peers = [(me_s, sibling)]
    peers += [(me_s, chip_at(i)) for i in range(1, n_chips)]
    peers += [(section_at(i), me_d) for i in range(1, n_sec)]
    for peer in peers:
        pl.semaphore_signal(barrier, inc=1, device_id=peer, device_id_type=MESH)

    loads = []
    for c in range(CHUNKS):
        span = pl.ds(c * cols, cols)
        four = []
        for k, (src, dst) in enumerate(((p_in, pi_v), (acts, a_v), (p_out, po_v), (grads, g_v))):
            load = pltpu.make_async_copy(src.at[:, span], dst.at[:, span], load_sem.at[c, k])
            load.start()
            four.append(load)
        loads.append(four)
    own = pltpu.make_async_copy(queries, q_v.at[me_d], own_sem)
    own.start()
    len_load = pltpu.make_async_copy(lengths, len_s, len_sem)
    len_load.start()

    pl.semaphore_wait(barrier, len(peers))

    def remote(src, dst, send, recv, device):
        return pltpu.make_async_remote_copy(
            src_ref=src, dst_ref=dst, send_sem=send, recv_sem=recv,
            device_id=device, device_id_type=MESH,
        )

    far_out = []
    for i in range(1, n_chips):
        for p in range(PIECES):
            span = pl.ds(p * piece, piece)
            copy = remote(
                queries.at[:, span], q_v.at[me_d, :, span],
                far_send.at[i - 1, p], far_recv.at[i - 1, p], (me_s, chip_at(i)),
            )
            copy.start()
            far_out.append(copy)
    to_sibling = remote(queries, q_v.at[me_d], sib_send, sib_recv, (me_s, sibling))
    to_sibling.start()

    fwd_out = []

    def forward(i, p):
        span = pl.ds(p * piece, piece)
        here = q_v.at[chip_at(-i), :, span]
        remote(
            queries.at[:, span], here,
            far_send.at[i - 1, p], far_recv.at[i - 1, p], (me_s, chip_at(i)),
        ).wait_recv()
        copy = remote(
            here, here, fwd_send.at[i - 1, p], fwd_recv.at[i - 1, p], (me_s, sibling)
        )
        copy.start()
        fwd_out.append(copy)

    in_acc = jnp.zeros((rows, rank), jnp.float32)
    out_acc = jnp.zeros((rank, rows), jnp.float32)
    for c in range(CHUNKS):
        span = pl.ds(c * cols, cols)
        loads[c][0].wait()
        loads[c][1].wait()
        in_acc += lax.dot_general(
            a_v[:, span], pi_v[:, span], NT, preferred_element_type=jnp.float32
        )
        loads[c][2].wait()
        loads[c][3].wait()
        out_acc += lax.dot_general(
            po_v[:, span], g_v[:, span], NT, preferred_element_type=jnp.float32
        )

    len_load.wait()
    token = lax.broadcasted_iota(jnp.int32, (rank, rows), 1)
    out_t = out_acc.astype(jnp.bfloat16).astype(jnp.float32)
    blocks = []
    for e in range(n_ex):
        keep = (token >= e * slots) & (token < e * slots + len_s[0, e])
        blocks.append(jnp.where(keep, out_t, 0.0))
    spread = jnp.concatenate(blocks, axis=0).astype(jnp.bfloat16)
    in_c = in_acc.astype(jnp.bfloat16)
    twice = jnp.concatenate([in_c, in_c], axis=1)
    proj = jnp.dot(spread, twice, preferred_element_type=jnp.float32)
    rows_v[...] = proj.astype(jnp.bfloat16).astype(jnp.float32)

    for i in range(1, n_chips):
        for p in range(PIECES):
            forward(i, p)

    low = lax.broadcasted_iota(jnp.int32, (n_ex, 2 * rank), 1) < rank
    parts = []
    for j in range(0, rank, 2):
        even = rows_v[pl.ds(j, n_ex, stride=rank), :]
        odd = rows_v[pl.ds(j + 1, n_ex, stride=rank), :]
        parts.append(jnp.where(low, even, odd))
    flat = jnp.concatenate(parts, axis=1).astype(jnp.bfloat16)

    own.wait()
    remote(queries, q_v.at[sibling], sib_send, sib_recv, (me_s, sibling)).wait_recv()
    for i in range(1, n_chips):
        for p in range(PIECES):
            span = pl.ds(p * piece, piece)
            there = q_v.at[lax.rem(chip - i + n_chips, n_chips) * 2 + 1 - core, :, span]
            remote(there, there, fwd_send.at[i - 1, p], fwd_recv.at[i - 1, p], (me_s, sibling)).wait_recv()
    all_q = q_v[...].reshape(q_v.shape[0] * q_v.shape[1], depth)
    part = lax.dot_general(flat, all_q, NT, preferred_element_type=jnp.float32)
    part_v[...] = part
    recv_v[me_s] = part

    sum_out = []
    for i in range(1, n_sec):
        copy = remote(
            part_v, recv_v.at[me_s], sum_send.at[i - 1], sum_recv.at[i - 1], (section_at(i), me_d)
        )
        copy.start()
        sum_out.append(copy)
    for i in range(1, n_sec):
        remote(
            part_v, recv_v.at[section_at(-i)], sum_send.at[i - 1], sum_recv.at[i - 1],
            (section_at(i), me_d),
        ).wait_recv()
    total = recv_v[0]
    for s in range(1, n_sec):
        total += recv_v[s]
    out[...] = total
    for copy in far_out + [to_sibling] + fwd_out + sum_out:
        copy.wait_send()


def solution(mesh):
    n_sec, n_dp = mesh.shape["section"], mesh.shape["dp"]
    placed = (
        P("section", "dp", None, None),
        P("section", "dp", None, None),
        P("section", None, None),
        P("section", None, None),
        P("section", "dp", None),
        P("dp", None),
    )

    def body(activations, out_grads, proj_in, proj_out, queries, lengths):
        n_ex, slots, width = activations.shape[1:]
        rank = proj_in.shape[1]
        n_q, depth = queries.shape[1:]
        rows = n_ex * slots
        n_far = max(n_dp // 2 - 1, 1)
        bf16, f32 = jnp.bfloat16, jnp.float32
        dma = pltpu.SemaphoreType.DMA
        hbm = pl.BlockSpec(memory_space=pl.ANY)
        scores = pl.pallas_call(
            functools.partial(kernel, n_sec, n_dp, n_ex),
            out_shape=jax.ShapeDtypeStruct((n_ex, n_dp * n_q), f32),
            in_specs=[hbm] * 6,
            out_specs=pl.BlockSpec(memory_space=pltpu.VMEM),
            scratch_shapes=[
                pltpu.VMEM((rows, width), bf16),
                pltpu.VMEM((rows, width), bf16),
                pltpu.VMEM((rank, width), bf16),
                pltpu.VMEM((rank, width), bf16),
                pltpu.VMEM((n_dp, n_q, depth), bf16),
                pltpu.SMEM(lengths.shape, jnp.int32),
                pltpu.VMEM((n_ex * rank, 2 * rank), f32),
                pltpu.VMEM((n_ex, n_dp * n_q), f32),
                pltpu.VMEM((n_sec, n_ex, n_dp * n_q), f32),
                dma((CHUNKS, 4)),
                dma,
                dma,
                dma((n_far, PIECES)),
                dma((n_far, PIECES)),
                dma((n_far, PIECES)),
                dma((n_far, PIECES)),
                dma,
                dma,
                dma((n_sec - 1,)),
                dma((n_sec - 1,)),
            ],
            compiler_params=pltpu.CompilerParams(
                collective_id=0, has_side_effects=True, vmem_limit_bytes=48 * 2**20
            ),
            cost_estimate=pl.CostEstimate(
                flops=4 * rows * width * rank,
                bytes_accessed=4 * (rows + rank) * width,
                transcendentals=0,
            ),
        )(
            activations.reshape(rows, width),
            out_grads.reshape(rows, width),
            proj_in[0],
            proj_out[0],
            queries[0],
            lengths,
        )
        norm_factor = 1.0 / (rank * (slots * n_sec) ** 0.5)
        return scores * norm_factor

    return jax.shard_map(body, mesh=mesh, in_specs=placed, out_specs=P("dp", None), check_vma=False)
```

time: 45.3 us -> 20.4 us (0.45)
  blocking collectives: 35.2 us -> 0 us
  Pallas kernels: 0 us -> 15.6 us
  matrix products: 7.55 us -> 0 us
  local copies, waits for them, and re-layouts: 1.41 us -> 4.01 us
    psum x1 -> x0, blocking collectives: 22.3 us -> none  [body(): layer_scores = lax.psum(partial_scores, 'section')]
    pallas_call x0 -> x1, Pallas kernels: none -> 15.6 us  [body(): pl.pallas_call(functools.partial(kernel, n_sec, n_dp, n_ex), out_shape=ja...]
    dot_general x4 -> x0, matrix products: 7.55 us -> none  [the longest x1 3.58 us: body(): jnp.dot(layer_grads.reshape(-1, width), proj_out[0].T, preferred_element_...]
    all_gather x1 -> x0, blocking collectives: 6.51 us -> none  [body(): all_grads = lax.all_gather(projected, 'dp', axis=0, tiled=True)]
    all_to_all x1 -> x0, blocking collectives: 6.4 us -> none  [body(): lax.all_to_all(layer_scores, 'dp', split_axis=0, concat_axis=1, tiled=True)]
    unnamed x8, local copies, waits for them, and re-layouts: 0.52 us -> 4.01 us
    convert_element_type x1 -> x0, other arithmetic: 0.87 us -> none  [body(): (positions[None, :] < lengths_flat[:, None]).astype(jnp.bfloat16)]
    mul x2 -> x0, local copies, waits for them, and re-layouts: 0.67 us -> none  [body(): return summed_scores * norm_factor]
where the time goes in v1:
time: 20.4 us; the launch traced here: 20.2 us
  Pallas kernels  15.6 us (76%)
  local copies, waits for them, and re-layouts  4.01 us (20%)
  other arithmetic  0.58 us (3%)
    pallas_call x1, Pallas kernels, body(): pl.pallas_call(functools.partial(kernel, n_sec, n_dp, n_ex), out_shape=ja...  15.6 us
    unnamed x8, local copies, waits for them, and re-layouts  4.01 us
    mul x1, other arithmetic, body(): return scores * norm_factor  0.58 us

profile of v1, /device:TPU:0, one launch (start us, length us, event | category | flops | bytes accessed | tf_op | source)
XLA Modules:
  0.0 20.2 jit_solution(4421944746325089732)
XLA Ops:
  0.0 0.0 copy-start
  0.0 1.2 %copy-done = bf16[1,64,8192]{2,1,0:T(8,128)(2,1)S(1)} copy-done((bf16[1,64,8192]{2,1,0:T(8,128)(2,1)S(1)}, bf16[1,64,8192]{2,1,0:T(8,128)(2,1)}, u32[]{:S(2)}) %copy-start) | copy-done | bytes 1048600
  1.2 0.0 copy-start.1
  1.2 1.2 %copy-done.1 = bf16[1,64,8192]{2,1,0:T(8,128)(2,1)S(1)} copy-done((bf16[1,64,8192]{2,1,0:T(8,128)(2,1)S(1)}, bf16[1,64,8192]{2,1,0:T(8,128)(2,1)}, u32[]{:S(2)}) %copy-start.1) | copy-done | bytes 1048600
  2.5 0.0 copy-start.2
  2.5 0.9 %copy-done.2 = bf16[1,16,4096]{2,1,0:T(8,128)(2,1)S(1)} copy-done((bf16[1,16,4096]{2,1,0:T(8,128)(2,1)S(1)}, bf16[1,16,4096]{2,1,0:T(8,128)(2,1)}, u32[]{:S(2)}) %copy-start.2) | copy-done | bytes 131096
  3.4 0.0 copy-start.3
  3.4 0.7 %copy-done.3 = s32[1,4]{1,0:T(1,128)S(1)} copy-done((s32[1,4]{1,0:T(1,128)S(1)}, s32[1,4]{1,0:T(1,128)}, u32[]{:S(2)}) %copy-start.3) | copy-done | bytes 40
  4.0 15.6 %shard_map.64 = f32[4,64]{1,0:T(4,128)S(1)} custom-call(bf16[256,8192]{1,0:T(8,128)(2,1)} %bitcast.8, bf16[256,8192]{1,0:T(8,128)(2,1)} %bitcast.9, bf16[64,8192]{1,0:T(8,128)(2,1)S(1)} %bitcast.5, bf16[64,8192]{1,0:T(8,128)(2,1)S(1)} %bitcast.6, bf16[16,4096]{1,0:T(8,128)(2,1)S(1)} %bitcast.7, s32[1,4]{1,0:T(1,128)S(1)} %copy-done.3), custom_call_target="tpu_custom_call" | custom-call | flops 536870912 | bytes 10485760 | tf_op jit(solution)/shard_map/pallas_call | solution.py:190
  19.7 0.6 %broadcast_multiply_fusion = f32[4,64]{1,0:T(4,128)} fusion(f32[4,64]{1,0:T(4,128)S(1)} %shard_map.64), kind=kLoop, calls=%fused_computation | loop fusion | flops 256 | bytes 2048 | tf_op jit(solution)/shard_map/mul | solution.py:234
Async XLA Ops:
  0.0 1.2 %copy-start = (bf16[1,64,8192]{2,1,0:T(8,128)(2,1)S(1)}, bf16[1,64,8192]{2,1,0:T(8,128)(2,1)}, u32[]{:S(2)}) copy-start(bf16[1,64,8192]{2,1,0:T(8,128)(2,1)} %param.8) | copy-start | bytes 3145732
  1.2 1.2 %copy-start.1 = (bf16[1,64,8192]{2,1,0:T(8,128)(2,1)S(1)}, bf16[1,64,8192]{2,1,0:T(8,128)(2,1)}, u32[]{:S(2)}) copy-start(bf16[1,64,8192]{2,1,0:T(8,128)(2,1)} %param.9) | copy-start | bytes 3145732
  2.5 0.9 %copy-start.2 = (bf16[1,16,4096]{2,1,0:T(8,128)(2,1)S(1)}, bf16[1,16,4096]{2,1,0:T(8,128)(2,1)}, u32[]{:S(2)}) copy-start(bf16[1,16,4096]{2,1,0:T(8,128)(2,1)} %param.10) | copy-start | bytes 393220
  3.4 0.7 %copy-start.3 = (s32[1,4]{1,0:T(1,128)S(1)}, s32[1,4]{1,0:T(1,128)}, u32[]{:S(2)}) copy-start(s32[1,4]{1,0:T(1,128)} %lengths.1) | copy-start | bytes 52

commit v2 on v1

--- a/solution.py
+++ b/solution.py
@@ -8,7 +8,7 @@
 from jax.sharding import PartitionSpec as P
 
 MESH = pl.DeviceIdType.MESH
-CHUNKS = 8
+CHUNKS = 4
 PIECES = 2
 NT = (((1,), (1,)), ((), ()))
 
@@ -95,24 +95,27 @@
         copy.start()
         fwd_out.append(copy)
 
-    in_acc = jnp.zeros((rows, rank), jnp.float32)
-    out_acc = jnp.zeros((rank, rows), jnp.float32)
+    halves = [pl.ds(h * (rows // 2), rows // 2) for h in range(2)]
+    in_acc, out_acc = [None] * 2, [None] * 2
     for c in range(CHUNKS):
         span = pl.ds(c * cols, cols)
-        loads[c][0].wait()
-        loads[c][1].wait()
-        in_acc += lax.dot_general(
-            a_v[:, span], pi_v[:, span], NT, preferred_element_type=jnp.float32
-        )
-        loads[c][2].wait()
-        loads[c][3].wait()
-        out_acc += lax.dot_general(
-            po_v[:, span], g_v[:, span], NT, preferred_element_type=jnp.float32
-        )
+        for load in loads[c]:
+            load.wait()
+        for h, half in enumerate(halves):
+            in_part = lax.dot_general(
+                a_v[half, span], pi_v[:, span], NT, preferred_element_type=jnp.float32
+            )
+            out_part = lax.dot_general(
+                g_v[half, span], po_v[:, span], NT, preferred_element_type=jnp.float32
+            )
+            in_acc[h] = in_part if c == 0 else in_acc[h] + in_part
+            out_acc[h] = out_part if c == 0 else out_acc[h] + out_part
+    in_acc = jnp.concatenate(in_acc, axis=0)
+    out_acc = jnp.concatenate(out_acc, axis=0)
 
     len_load.wait()
     token = lax.broadcasted_iota(jnp.int32, (rank, rows), 1)
-    out_t = out_acc.astype(jnp.bfloat16).astype(jnp.float32)
+    out_t = out_acc.astype(jnp.bfloat16).astype(jnp.float32).T
     blocks = []
     for e in range(n_ex):
         keep = (token >= e * slots) & (token < e * slots + len_s[0, e])
@@ -215,7 +218,7 @@
                 dma((n_sec - 1,)),
             ],
             compiler_params=pltpu.CompilerParams(
-                collective_id=0, has_side_effects=True, vmem_limit_bytes=48 * 2**20
+                collective_id=0, has_side_effects=True, vmem_limit_bytes=63 * 2**20
             ),
             cost_estimate=pl.CostEstimate(
                 flops=4 * rows * width * rank,

time: 20.4 us -> 16.5 us (0.81)
  local copies, waits for them, and re-layouts: 4.01 us -> 0 us
  other arithmetic: 0.58 us -> 1.26 us
  Pallas kernels: 15.6 us -> 15.1 us
    unnamed x8 -> x0, local copies, waits for them, and re-layouts: 4.01 us -> none
    mul x1, other arithmetic: 0.58 us -> 1.26 us  [body(): return scores * norm_factor]
    pallas_call x1, Pallas kernels: 15.6 us -> 15.1 us  [body(): pl.pallas_call(functools.partial(kernel, n_sec, n_dp, n_ex), out_shape=ja...]
where the time goes in v2:
time: 16.5 us; the launch traced here: 16.4 us
  Pallas kernels  15.1 us (92%)
  other arithmetic  1.26 us (8%)
    pallas_call x1, Pallas kernels, body(): pl.pallas_call(functools.partial(kernel, n_sec, n_dp, n_ex), out_shape=ja...  15.1 us
    mul x1, other arithmetic, body(): return scores * norm_factor  1.26 us

profile of v2, /device:TPU:0, one launch (start us, length us, event | category | flops | bytes accessed | tf_op | source)
XLA Modules:
  0.0 16.4 jit_solution(3647613115683019925)
XLA Ops:
  0.0 15.1 %shard_map.64 = f32[4,64]{1,0:T(4,128)} custom-call(bf16[256,8192]{1,0:T(8,128)(2,1)} %bitcast.5, bf16[256,8192]{1,0:T(8,128)(2,1)} %bitcast.6, bf16[64,8192]{1,0:T(8,128)(2,1)} %bitcast.7, bf16[64,8192]{1,0:T(8,128)(2,1)} %bitcast.8, bf16[16,4096]{1,0:T(8,128)(2,1)} %bitcast.9, s32[1,4]{1,0:T(1,128)} %lengths.1), custom_call_target="tpu_custom_call" | custom-call | flops 536870912 | bytes 10485760 | tf_op jit(solution)/shard_map/pallas_call | solution.py:193
  15.1 1.3 %broadcast_multiply_fusion = f32[4,64]{1,0:T(4,128)} fusion(f32[4,64]{1,0:T(4,128)} %shard_map.64), kind=kLoop, calls=%fused_computation | loop fusion | flops 256 | bytes 2048 | tf_op jit(solution)/shard_map/mul | solution.py:237

commit v3 on v2

--- a/solution.py
+++ b/solution.py
@@ -59,8 +59,6 @@
     len_load = pltpu.make_async_copy(lengths, len_s, len_sem)
     len_load.start()
 
-    pl.semaphore_wait(barrier, len(peers))
-
     def remote(src, dst, send, recv, device):
         return pltpu.make_async_remote_copy(
             src_ref=src, dst_ref=dst, send_sem=send, recv_sem=recv,
@@ -68,17 +66,20 @@
         )
 
     far_out = []
-    for i in range(1, n_chips):
-        for p in range(PIECES):
-            span = pl.ds(p * piece, piece)
-            copy = remote(
-                queries.at[:, span], q_v.at[me_d, :, span],
-                far_send.at[i - 1, p], far_recv.at[i - 1, p], (me_s, chip_at(i)),
-            )
-            copy.start()
-            far_out.append(copy)
-    to_sibling = remote(queries, q_v.at[me_d], sib_send, sib_recv, (me_s, sibling))
-    to_sibling.start()
+
+    def send_queries():
+        for i in range(1, n_chips):
+            for p in range(PIECES):
+                span = pl.ds(p * piece, piece)
+                copy = remote(
+                    queries.at[:, span], q_v.at[me_d, :, span],
+                    far_send.at[i - 1, p], far_recv.at[i - 1, p], (me_s, chip_at(i)),
+                )
+                copy.start()
+                far_out.append(copy)
+        copy = remote(queries, q_v.at[me_d], sib_send, sib_recv, (me_s, sibling))
+        copy.start()
+        far_out.append(copy)
 
     fwd_out = []
 
@@ -110,6 +111,9 @@
             )
             in_acc[h] = in_part if c == 0 else in_acc[h] + in_part
             out_acc[h] = out_part if c == 0 else out_acc[h] + out_part
+        if c == 0:
+            pl.semaphore_wait(barrier, len(peers))
+            send_queries()
     in_acc = jnp.concatenate(in_acc, axis=0)
     out_acc = jnp.concatenate(out_acc, axis=0)
 
@@ -166,7 +170,7 @@
     for s in range(1, n_sec):
         total += recv_v[s]
     out[...] = total
-    for copy in far_out + [to_sibling] + fwd_out + sum_out:
+    for copy in far_out + fwd_out + sum_out:
         copy.wait_send()
 
 

time: 16.5 us -> 17.5 us (1.061)
  Pallas kernels: 15.1 us -> 16.1 us
    pallas_call x1, Pallas kernels: 15.1 us -> 16.1 us  [body(): pl.pallas_call(functools.partial(kernel, n_sec, n_dp, n_ex), out_shape=ja...]
where the time goes in v3:
time: 17.5 us; the launch traced here: 17.4 us
  Pallas kernels  16.1 us (92%)
  other arithmetic  1.26 us (7%)
    pallas_call x1, Pallas kernels, body(): pl.pallas_call(functools.partial(kernel, n_sec, n_dp, n_ex), out_shape=ja...  16.1 us
    mul x1, other arithmetic, body(): return scores * norm_factor  1.26 us

profile of v3, /device:TPU:0, one launch (start us, length us, event | category | flops | bytes accessed | tf_op | source)
XLA Modules:
  0.0 17.4 jit_solution(12802782359357464301)
XLA Ops:
  0.0 16.1 %shard_map.64 = f32[4,64]{1,0:T(4,128)} custom-call(bf16[256,8192]{1,0:T(8,128)(2,1)} %bitcast.5, bf16[256,8192]{1,0:T(8,128)(2,1)} %bitcast.6, bf16[64,8192]{1,0:T(8,128)(2,1)} %bitcast.7, bf16[64,8192]{1,0:T(8,128)(2,1)} %bitcast.8, bf16[16,4096]{1,0:T(8,128)(2,1)} %bitcast.9, s32[1,4]{1,0:T(1,128)} %lengths.1), custom_call_target="tpu_custom_call" | custom-call | flops 536870912 | bytes 10485760 | tf_op jit(solution)/shard_map/pallas_call | solution.py:197
  16.1 1.3 %broadcast_multiply_fusion = f32[4,64]{1,0:T(4,128)} fusion(f32[4,64]{1,0:T(4,128)} %shard_map.64), kind=kLoop, calls=%fused_computation | loop fusion | flops 256 | bytes 2048 | tf_op jit(solution)/shard_map/mul | solution.py:241

commit v4 on v1

--- a/solution.py
+++ b/solution.py
@@ -16,7 +16,7 @@
 def kernel(
     n_sec, n_dp, n_ex,
     acts, grads, p_in, p_out, queries, lengths, out,
-    a_v, g_v, pi_v, po_v, q_v, len_s, rows_v, part_v, recv_v,
+    a_v, g_v, pi_v, po_v, q_v, len_s, rows_v, blocks_v, part_v, recv_v,
     load_sem, own_sem, len_sem, far_send, far_recv, fwd_send, fwd_recv,
     sib_send, sib_recv, sum_send, sum_recv,
 ):
@@ -95,20 +95,23 @@
         copy.start()
         fwd_out.append(copy)
 
-    in_acc = jnp.zeros((rows, rank), jnp.float32)
-    out_acc = jnp.zeros((rank, rows), jnp.float32)
-    for c in range(CHUNKS):
-        span = pl.ds(c * cols, cols)
-        loads[c][0].wait()
-        loads[c][1].wait()
-        in_acc += lax.dot_general(
-            a_v[:, span], pi_v[:, span], NT, preferred_element_type=jnp.float32
-        )
-        loads[c][2].wait()
-        loads[c][3].wait()
-        out_acc += lax.dot_general(
-            po_v[:, span], g_v[:, span], NT, preferred_element_type=jnp.float32
-        )
+    def project(in_mxu, out_mxu):
+        for c in range(CHUNKS):
+            for load in loads[c]:
+                load.wait()
+            for t in range(cols // rows):
+                span = pl.ds(c * cols + t * rows, rows)
+                stage = t % 2
+                pltpu.matmul_push_rhs(a_v[:, span], stage, 0, transpose=True)
+                pltpu.matmul_push_rhs(g_v[:, span], stage, 1, transpose=True)
+                pltpu.matmul_acc_lhs(in_mxu, pi_v[:, span], stage)
+                pltpu.matmul_acc_lhs(out_mxu, po_v[:, span], stage)
+        return pltpu.matmul_pop(in_mxu), pltpu.matmul_pop(out_mxu)
+
+    sums = (rank, rows)
+    in_acc, out_acc = pl.run_scoped(
+        project, pltpu.ACC(0)(sums, jnp.float32), pltpu.ACC(1)(sums, jnp.float32)
+    )
 
     len_load.wait()
     token = lax.broadcasted_iota(jnp.int32, (rank, rows), 1)
@@ -119,21 +122,25 @@
         blocks.append(jnp.where(keep, out_t, 0.0))
     spread = jnp.concatenate(blocks, axis=0).astype(jnp.bfloat16)
     in_c = in_acc.astype(jnp.bfloat16)
-    twice = jnp.concatenate([in_c, in_c], axis=1)
-    proj = jnp.dot(spread, twice, preferred_element_type=jnp.float32)
-    rows_v[...] = proj.astype(jnp.bfloat16).astype(jnp.float32)
+    fill = jnp.concatenate([in_c] * (rows // rank), axis=0)
+    half = n_ex * rank // 2
+
+    def outer(low_mxu, high_mxu):
+        for unit, acc in enumerate((low_mxu, high_mxu)):
+            pltpu.matmul_push_rhs(fill, 0, unit, transpose=True)
+            pltpu.matmul_acc_lhs(acc, spread[unit * half:(unit + 1) * half], 0)
+        return pltpu.matmul_pop(low_mxu), pltpu.matmul_pop(high_mxu)
+
+    sums = (half, rows)
+    proj = pl.run_scoped(outer, pltpu.ACC(0)(sums, jnp.float32), pltpu.ACC(1)(sums, jnp.float32))
+    for unit in range(2):
+        rows_v[pl.ds(unit * half, half), :] = (
+            proj[unit][:, :2 * rank].astype(jnp.bfloat16).astype(jnp.float32)
+        )
 
     for i in range(1, n_chips):
         for p in range(PIECES):
             forward(i, p)
-
-    low = lax.broadcasted_iota(jnp.int32, (n_ex, 2 * rank), 1) < rank
-    parts = []
-    for j in range(0, rank, 2):
-        even = rows_v[pl.ds(j, n_ex, stride=rank), :]
-        odd = rows_v[pl.ds(j + 1, n_ex, stride=rank), :]
-        parts.append(jnp.where(low, even, odd))
-    flat = jnp.concatenate(parts, axis=1).astype(jnp.bfloat16)
 
     own.wait()
     remote(queries, q_v.at[sibling], sib_send, sib_recv, (me_s, sibling)).wait_recv()
@@ -142,8 +149,43 @@
             span = pl.ds(p * piece, piece)
             there = q_v.at[lax.rem(chip - i + n_chips, n_chips) * 2 + 1 - core, :, span]
             remote(there, there, fwd_send.at[i - 1, p], fwd_recv.at[i - 1, p], (me_s, sibling)).wait_recv()
-    all_q = q_v[...].reshape(q_v.shape[0] * q_v.shape[1], depth)
-    part = lax.dot_general(flat, all_q, NT, preferred_element_type=jnp.float32)
+    n_q = q_v.shape[0] * q_v.shape[1]
+    per = rows // n_q
+    lines = n_ex * per
+    low = lax.broadcasted_iota(jnp.int32, (lines, 2 * rank), 1) < rank
+    in_tile = rows // rank
+
+    def score(even_mxu, odd_mxu):
+        accs = (even_mxu, odd_mxu)
+        for g in range(rank // in_tile // per):
+            left = []
+            for h in range(0, in_tile, 2):
+                even = rows_v[pl.ds(g * in_tile + h, lines, stride=rank // per), :]
+                odd = rows_v[pl.ds(g * in_tile + h + 1, lines, stride=rank // per), :]
+                left.append(jnp.where(low, even, odd))
+            left = jnp.concatenate(left, axis=1)
+            if lines < 16:
+                left = jnp.concatenate([left, jnp.zeros((16 - lines, rows), left.dtype)], axis=0)
+            tile = [
+                q_v[:, :, pl.ds(b * (depth // per) + g * rows, rows)].reshape(n_q, rows)
+                for b in range(per)
+            ]
+            unit, stage = g % 2, (g // 2) % 2
+            pltpu.matmul_push_rhs(jnp.concatenate(tile, axis=0), stage, unit, transpose=True)
+            pltpu.matmul_acc_lhs(accs[unit], left.astype(jnp.bfloat16), stage)
+        return pltpu.matmul_pop(even_mxu) + pltpu.matmul_pop(odd_mxu)
+
+    sums = (max(lines, 16), rows)
+    blocks = pl.run_scoped(
+        score, pltpu.ACC(0)(sums, jnp.float32), pltpu.ACC(1)(sums, jnp.float32)
+    )
+    lanes = blocks_v.shape[2]
+    for h in range(rows // lanes):
+        blocks_v[h] = blocks[:, h * lanes:(h + 1) * lanes]
+    part = jnp.zeros((n_ex, n_q), jnp.float32)
+    for b in range(per):
+        line = [blocks_v[h, pl.ds(b, n_ex, stride=per), :] for h in range(rows // lanes)]
+        part += jnp.concatenate(line, axis=1)[:, b * n_q:(b + 1) * n_q]
     part_v[...] = part
     recv_v[me_s] = part
 
@@ -200,6 +242,7 @@
                 pltpu.VMEM((n_dp, n_q, depth), bf16),
                 pltpu.SMEM(lengths.shape, jnp.int32),
                 pltpu.VMEM((n_ex * rank, 2 * rank), f32),
+                pltpu.VMEM((rows // 128, max(n_ex * rows // (n_dp * n_q), 16), 128), f32),
                 pltpu.VMEM((n_ex, n_dp * n_q), f32),
                 pltpu.VMEM((n_sec, n_ex, n_dp * n_q), f32),
                 dma((CHUNKS, 4)),
@@ -215,7 +258,7 @@
                 dma((n_sec - 1,)),
             ],
             compiler_params=pltpu.CompilerParams(
-                collective_id=0, has_side_effects=True, vmem_limit_bytes=48 * 2**20
+                collective_id=0, has_side_effects=True, vmem_limit_bytes=63 * 2**20
             ),
             cost_estimate=pl.CostEstimate(
                 flops=4 * rows * width * rank,

time: 20.4 us -> 16.6 us (0.81)
  local copies, waits for them, and re-layouts: 4.01 us -> 0 us
  other arithmetic: 0.58 us -> 1.26 us
  Pallas kernels: 15.6 us -> 15.2 us
    unnamed x8 -> x0, local copies, waits for them, and re-layouts: 4.01 us -> none
    mul x1, other arithmetic: 0.58 us -> 1.26 us  [body(): return scores * norm_factor]
    pallas_call x1, Pallas kernels: 15.6 us -> 15.2 us  [body(): pl.pallas_call(functools.partial(kernel, n_sec, n_dp, n_ex), out_shape=ja...]
where the time goes in v4:
time: 16.6 us; the launch traced here: 16.4 us
  Pallas kernels  15.2 us (92%)
  other arithmetic  1.26 us (8%)
    pallas_call x1, Pallas kernels, body(): pl.pallas_call(functools.partial(kernel, n_sec, n_dp, n_ex), out_shape=ja...  15.2 us
    mul x1, other arithmetic, body(): return scores * norm_factor  1.26 us

profile of v4, /device:TPU:0, one launch (start us, length us, event | category | flops | bytes accessed | tf_op | source)
XLA Modules:
  0.0 16.4 jit_solution(2390481187205555124)
XLA Ops:
  0.0 15.2 %shard_map.64 = f32[4,64]{1,0:T(4,128)} custom-call(bf16[256,8192]{1,0:T(8,128)(2,1)} %bitcast.5, bf16[256,8192]{1,0:T(8,128)(2,1)} %bitcast.6, bf16[64,8192]{1,0:T(8,128)(2,1)} %bitcast.7, bf16[64,8192]{1,0:T(8,128)(2,1)} %bitcast.8, bf16[16,4096]{1,0:T(8,128)(2,1)} %bitcast.9, s32[1,4]{1,0:T(1,128)} %lengths.1), custom_call_target="tpu_custom_call" | custom-call | flops 536870912 | bytes 10485760 | tf_op jit(solution)/shard_map/pallas_call | solution.py:232
  15.2 1.3 %broadcast_multiply_fusion = f32[4,64]{1,0:T(4,128)} fusion(f32[4,64]{1,0:T(4,128)} %shard_map.64), kind=kLoop, calls=%fused_computation | loop fusion | flops 256 | bytes 2048 | tf_op jit(solution)/shard_map/mul | solution.py:277

commit v5 on v4

v5 whole, which is shorter than its diff:
```python
import functools

import jax
import jax.numpy as jnp
from jax import lax
from jax.experimental import pallas as pl
from jax.experimental.pallas import tpu as pltpu
from jax.sharding import PartitionSpec as P

MESH = pl.DeviceIdType.MESH
CHUNKS = 8
NT = (((1,), (1,)), ((), ()))


def kernel(
    n_sec, n_dp, n_ex,
    acts, grads, p_in, p_out, queries, lengths, out,
    a_v, g_v, pi_v, po_v, q_v, len_s, rows_v, left_v, part_v, recv_v,
    load_sem, own_sem, len_sem, sib_send, sib_recv, left_send, left_recv, sum_send, sum_recv,
):
    me_s, me_d = lax.axis_index("section"), lax.axis_index("dp")
    n_chips = n_dp // 2
    chip, core = me_d // 2, lax.rem(me_d, 2)
    sibling = chip * 2 + 1 - core

    def chip_at(step):
        return lax.rem(chip + step + n_chips, n_chips)

    def dp_at(step):
        return chip_at(step) * 2 + core

    def section_at(step):
        return lax.rem(me_s + step + n_sec, n_sec)

    rows, width = acts.shape
    rank = p_in.shape[0]
    slots = rows // n_ex
    depth = queries.shape[1]
    cols = width // CHUNKS
    others = [(k, i) for i in range(n_chips) for k in range(n_sec) if (k, i) != (0, 0)]

    barrier = pltpu.get_barrier_semaphore()
    peers = [(me_s, sibling)] + [(section_at(k), dp_at(i)) for k, i in others]
    for peer in peers:
        pl.semaphore_signal(barrier, inc=1, device_id=peer, device_id_type=MESH)

    loads = []
    for c in range(CHUNKS):
        span = pl.ds(c * cols, cols)
        four = []
        for k, (src, dst) in enumerate(((p_in, pi_v), (acts, a_v), (p_out, po_v), (grads, g_v))):
            load = pltpu.make_async_copy(src.at[:, span], dst.at[:, span], load_sem.at[c, k])
            load.start()
            four.append(load)
        loads.append(four)
    own = pltpu.make_async_copy(queries, q_v.at[core], own_sem)
    own.start()
    len_load = pltpu.make_async_copy(lengths, len_s, len_sem)
    len_load.start()

    def remote(src, dst, send, recv, device):
        return pltpu.make_async_remote_copy(
            src_ref=src, dst_ref=dst, send_sem=send, recv_sem=recv,
            device_id=device, device_id_type=MESH,
        )

    to_sibling = remote(queries, q_v.at[core], sib_send, sib_recv, (me_s, sibling))

    def project(in_mxu, out_mxu):
        for c in range(CHUNKS):
            if c == CHUNKS // 2:
                pl.semaphore_wait(barrier, len(peers))
                to_sibling.start()
            for load in loads[c]:
                load.wait()
            for t in range(cols // rows):
                span = pl.ds(c * cols + t * rows, rows)
                stage = t % 2
                pltpu.matmul_push_rhs(a_v[:, span], stage, 0, transpose=True)
                pltpu.matmul_push_rhs(g_v[:, span], stage, 1, transpose=True)
                pltpu.matmul_acc_lhs(in_mxu, pi_v[:, span], stage)
                pltpu.matmul_acc_lhs(out_mxu, po_v[:, span], stage)
        return pltpu.matmul_pop(in_mxu), pltpu.matmul_pop(out_mxu)

    sums = (rank, rows)
    in_acc, out_acc = pl.run_scoped(
        project, pltpu.ACC(0)(sums, jnp.float32), pltpu.ACC(1)(sums, jnp.float32)
    )

    len_load.wait()
    token = lax.broadcasted_iota(jnp.int32, (rank, rows), 1)
    out_t = out_acc.astype(jnp.bfloat16).astype(jnp.float32)
    blocks = []
    for e in range(n_ex):
        keep = (token >= e * slots) & (token < e * slots + len_s[0, e])
        blocks.append(jnp.where(keep, out_t, 0.0))
    spread = jnp.concatenate(blocks, axis=0).astype(jnp.bfloat16)
    fill = jnp.concatenate([in_acc.astype(jnp.bfloat16)] * (rows // rank), axis=0)
    half = n_ex * rank // 2

    def outer(low_mxu, high_mxu):
        for unit, acc in enumerate((low_mxu, high_mxu)):
            pltpu.matmul_push_rhs(fill, 0, unit, transpose=True)
            pltpu.matmul_acc_lhs(acc, spread[unit * half:(unit + 1) * half], 0)
        return pltpu.matmul_pop(low_mxu), pltpu.matmul_pop(high_mxu)

    sums = (half, rows)
    proj = pl.run_scoped(outer, pltpu.ACC(0)(sums, jnp.float32), pltpu.ACC(1)(sums, jnp.float32))
    for unit in range(2):
        rows_v[pl.ds(unit * half, half), :] = (
            proj[unit][:, :2 * rank].astype(jnp.bfloat16).astype(jnp.float32)
        )

    n_q = q_v.shape[0] * q_v.shape[1]
    per = rows // n_q
    lines = n_ex * per
    in_tile = rows // rank
    groups = left_v.shape[1]
    low = lax.broadcasted_iota(jnp.int32, (lines, 2 * rank), 1) < rank
    for g in range(groups):
        for h in range(0, in_tile, 2):
            even = rows_v[pl.ds(g * in_tile + h, lines, stride=rank // per), :]
            odd = rows_v[pl.ds(g * in_tile + h + 1, lines, stride=rank // per), :]
            left_v[0, g, :, pl.ds(h * rank, 2 * rank)] = jnp.where(low, even, odd).astype(jnp.bfloat16)

    left_out = []
    for i in range(1, n_chips):
        copy = remote(
            left_v.at[0], left_v.at[i], left_send.at[i - 1], left_recv.at[i - 1], (me_s, dp_at(i))
        )
        copy.start()
        left_out.append(copy)

    own.wait()
    remote(queries, q_v.at[1 - core], sib_send, sib_recv, (me_s, sibling)).wait_recv()

    line = lax.broadcasted_iota(jnp.int32, (lines, rows), 0)
    column = lax.broadcasted_iota(jnp.int32, (lines, rows), 1)
    diagonal = lax.rem(line, per) == column // n_q

    sum_out = []

    def score(*accs):
        for i in range(n_chips):
            if i > 0:
                left_out[i - 1].wait_recv()
            for g in range(groups):
                unit = g % 2
                if groups > 2 or i == 0:
                    tile = [
                        q_v[:, :, pl.ds(b * (depth // per) + g * rows, rows)].reshape(n_q, rows)
                        for b in range(per)
                    ]
                    pltpu.matmul_push_rhs(jnp.concatenate(tile, axis=0), 0, unit, transpose=True)
                    pltpu.matmul_acc_lhs(accs[unit], left_v[i, g], 0)
                else:
                    pltpu.matmul_acc_lhs(accs[unit], left_v[i, g])
            full = pltpu.matmul_pop(accs[0]) + pltpu.matmul_pop(accs[1])
            part = jnp.where(diagonal, full, 0.0).reshape(n_ex, per, rows).sum(axis=1)
            wide = rows
            while wide > n_q:
                wide //= 2
                part = part[:, :wide] + part[:, wide:]
            part_v[i] = part
            if i == 0:
                recv_v[me_s, chip] = part
            for k in range(n_sec):
                if (k, i) != (0, 0):
                    copy = remote(
                        part_v.at[i], recv_v.at[me_s, chip], sum_send.at[k, i], sum_recv.at[k, i],
                        (section_at(k), dp_at(-i)),
                    )
                    copy.start()
                    sum_out.append(copy)

        for k, i in others:
            remote(
                part_v.at[i], recv_v.at[section_at(-k), chip_at(i)], sum_send.at[k, i], sum_recv.at[k, i],
                (section_at(k), dp_at(-i)),
            ).wait_recv()
        totals = []
        for c in range(n_chips):
            total = recv_v[0, c]
            for s in range(1, n_sec):
                total += recv_v[s, c]
            totals.append(total)
        out[...] = jnp.concatenate(totals, axis=1)
        for copy in [to_sibling] + left_out + sum_out:
            copy.wait_send()

    sums = (lines, rows)
    pl.run_scoped(score, pltpu.ACC(0)(sums, jnp.float32), pltpu.ACC(1)(sums, jnp.float32))


def solution(mesh):
    n_sec, n_dp = mesh.shape["section"], mesh.shape["dp"]
    placed = (
        P("section", "dp", None, None),
        P("section", "dp", None, None),
        P("section", None, None),
        P("section", None, None),
        P("section", "dp", None),
        P("dp", None),
    )

    def body(activations, out_grads, proj_in, proj_out, queries, lengths):
        n_ex, slots, width = activations.shape[1:]
        rank = proj_in.shape[1]
        n_q, depth = queries.shape[1:]
        rows = n_ex * slots
        n_chips = n_dp // 2
        per = rows // (2 * n_q)
        bf16, f32 = jnp.bfloat16, jnp.float32
        dma = pltpu.SemaphoreType.DMA
        hbm = pl.BlockSpec(memory_space=pl.ANY)
        scores = pl.pallas_call(
            functools.partial(kernel, n_sec, n_dp, n_ex),
            out_shape=jax.ShapeDtypeStruct((n_ex, n_dp * n_q), f32),
            in_specs=[hbm] * 6,
            out_specs=pl.BlockSpec(memory_space=pltpu.VMEM),
            scratch_shapes=[
                pltpu.VMEM((rows, width), bf16),
                pltpu.VMEM((rows, width), bf16),
                pltpu.VMEM((rank, width), bf16),
                pltpu.VMEM((rank, width), bf16),
                pltpu.VMEM((2, n_q, depth), bf16),
                pltpu.SMEM(lengths.shape, jnp.int32),
                pltpu.VMEM((n_ex * rank, 2 * rank), f32),
                pltpu.VMEM((n_chips, depth // (rows * per), n_ex * per, rows), bf16),
                pltpu.VMEM((n_chips, n_ex, 2 * n_q), f32),
                pltpu.VMEM((n_sec, n_chips, n_ex, 2 * n_q), f32),
                dma((CHUNKS, 4)),
                dma,
                dma,
                dma,
                dma,
                dma((max(n_chips - 1, 1),)),
                dma((max(n_chips - 1, 1),)),
                dma((n_sec, n_chips)),
                dma((n_sec, n_chips)),
            ],
            compiler_params=pltpu.CompilerParams(
                collective_id=0, has_side_effects=True, vmem_limit_bytes=63 * 2**20
            ),
            cost_estimate=pl.CostEstimate(
                flops=4 * rows * width * rank,
                bytes_accessed=4 * (rows + rank) * width,
                transcendentals=0,
            ),
        )(
            activations.reshape(rows, width),
            out_grads.reshape(rows, width),
            proj_in[0],
            proj_out[0],
            queries[0],
            lengths,
        )
        norm_factor = 1.0 / (rank * (slots * n_sec) ** 0.5)
        return scores * norm_factor

    return jax.shard_map(body, mesh=mesh, in_specs=placed, out_specs=P("dp", None), check_vma=False)
```

time: 16.6 us -> 18.7 us (1.13)
  Pallas kernels: 15.2 us -> 17.2 us
    pallas_call x1, Pallas kernels: 15.2 us -> 17.2 us  [body(): pl.pallas_call(functools.partial(kernel, n_sec, n_dp, n_ex), out_shape=ja...]
where the time goes in v5:
time: 18.7 us; the launch traced here: 18.5 us
  Pallas kernels  17.2 us (92%)
  other arithmetic  1.26 us (7%)
    pallas_call x1, Pallas kernels, body(): pl.pallas_call(functools.partial(kernel, n_sec, n_dp, n_ex), out_shape=ja...  17.2 us
    mul x1, other arithmetic, body(): return scores * norm_factor  1.26 us

profile of v5, /device:TPU:0, one launch (start us, length us, event | category | flops | bytes accessed | tf_op | source)
XLA Modules:
  0.0 18.5 jit_solution(3159461375777884236)
XLA Ops:
  0.0 17.2 %shard_map.64 = f32[4,64]{1,0:T(4,128)} custom-call(bf16[256,8192]{1,0:T(8,128)(2,1)} %bitcast.5, bf16[256,8192]{1,0:T(8,128)(2,1)} %bitcast.6, bf16[64,8192]{1,0:T(8,128)(2,1)} %bitcast.7, bf16[64,8192]{1,0:T(8,128)(2,1)} %bitcast.8, bf16[16,4096]{1,0:T(8,128)(2,1)} %bitcast.9, s32[1,4]{1,0:T(1,128)} %lengths.1), custom_call_target="tpu_custom_call" | custom-call | flops 536870912 | bytes 10485760 | tf_op jit(solution)/shard_map/pallas_call | solution.py:216
  17.3 1.3 %broadcast_multiply_fusion = f32[4,64]{1,0:T(4,128)} fusion(f32[4,64]{1,0:T(4,128)} %shard_map.64), kind=kLoop, calls=%fused_computation | loop fusion | flops 256 | bytes 2048 | tf_op jit(solution)/shard_map/mul | solution.py:259

commit v6 on v4

--- a/solution.py
+++ b/solution.py
@@ -9,16 +9,16 @@
 
 MESH = pl.DeviceIdType.MESH
 CHUNKS = 8
-PIECES = 2
+PIECES = 4
 NT = (((1,), (1,)), ((), ()))
 
 
 def kernel(
-    n_sec, n_dp, n_ex,
+    n_sec, n_dp, n_ex, norm_factor,
     acts, grads, p_in, p_out, queries, lengths, out,
     a_v, g_v, pi_v, po_v, q_v, len_s, rows_v, blocks_v, part_v, recv_v,
     load_sem, own_sem, len_sem, far_send, far_recv, fwd_send, fwd_recv,
-    sib_send, sib_recv, sum_send, sum_recv,
+    cross_send, cross_recv, sib_send, sib_recv, sum_send, sum_recv,
 ):
     me_s, me_d = lax.axis_index("section"), lax.axis_index("dp")
     n_chips = n_dp // 2
@@ -27,6 +27,9 @@
 
     def chip_at(step):
         return lax.rem(chip + step + n_chips, n_chips) * 2 + core
+
+    def across_at(step):
+        return lax.rem(chip + step + n_chips, n_chips) * 2 + 1 - core
 
     def section_at(step):
         return lax.rem(me_s + step + n_sec, n_sec)
@@ -41,6 +44,7 @@
     barrier = pltpu.get_barrier_semaphore()
     peers = [(me_s, sibling)]
     peers += [(me_s, chip_at(i)) for i in range(1, n_chips)]
+    peers += [(me_s, across_at(i)) for i in range(1, n_chips)]
     peers += [(section_at(i), me_d) for i in range(1, n_sec)]
     for peer in peers:
         pl.semaphore_signal(barrier, inc=1, device_id=peer, device_id_type=MESH)
@@ -67,33 +71,48 @@
             device_id=device, device_id_type=MESH,
         )
 
-    far_out = []
-    for i in range(1, n_chips):
-        for p in range(PIECES):
-            span = pl.ds(p * piece, piece)
+    pieces = [pl.ds(p * piece, piece) for p in range(PIECES)]
+    q_out, far_in, hand_on, cross_in = [], [], [], []
+    for p, span in enumerate(pieces):
+        for i in range(1, n_chips):
+            mine = q_v.at[me_d, :, span]
             copy = remote(
-                queries.at[:, span], q_v.at[me_d, :, span],
-                far_send.at[i - 1, p], far_recv.at[i - 1, p], (me_s, chip_at(i)),
+                queries.at[:, span], mine, far_send.at[i - 1, p], far_recv.at[i - 1, p], (me_s, chip_at(i))
             )
             copy.start()
-            far_out.append(copy)
+            q_out.append(copy)
+            if p == PIECES - 1:
+                copy = remote(
+                    queries.at[:, span], mine, cross_send.at[i - 1], cross_recv.at[i - 1], (me_s, across_at(i))
+                )
+                copy.start()
+                q_out.append(copy)
     to_sibling = remote(queries, q_v.at[me_d], sib_send, sib_recv, (me_s, sibling))
     to_sibling.start()
-
-    fwd_out = []
-
-    def forward(i, p):
-        span = pl.ds(p * piece, piece)
-        here = q_v.at[chip_at(-i), :, span]
-        remote(
-            queries.at[:, span], here,
-            far_send.at[i - 1, p], far_recv.at[i - 1, p], (me_s, chip_at(i)),
-        ).wait_recv()
-        copy = remote(
-            here, here, fwd_send.at[i - 1, p], fwd_recv.at[i - 1, p], (me_s, sibling)
-        )
-        copy.start()
-        fwd_out.append(copy)
+    for p, span in enumerate(pieces):
+        for i in range(1, n_chips):
+            here = q_v.at[chip_at(-i), :, span]
+            far_in.append(remote(
+                here, here, far_send.at[i - 1, p], far_recv.at[i - 1, p], (me_s, chip_at(i))
+            ))
+            if p < PIECES - 1:
+                hand_on.append(remote(
+                    here, here, fwd_send.at[i - 1, p], fwd_recv.at[i - 1, p], (me_s, sibling)
+                ))
+            there = q_v.at[across_at(-i), :, span]
+            if p < PIECES - 1:
+                cross_in.append(remote(
+                    there, there, fwd_send.at[i - 1, p], fwd_recv.at[i - 1, p], (me_s, sibling)
+                ))
+            else:
+                cross_in.append(remote(
+                    there, there, cross_send.at[i - 1], cross_recv.at[i - 1], (me_s, across_at(i))
+                ))
+
+    def forward(p):
+        for i in range(n_chips - 1):
+            far_in[p * (n_chips - 1) + i].wait_recv()
+            hand_on[p * (n_chips - 1) + i].start()
 
     def project(in_mxu, out_mxu):
         for c in range(CHUNKS):
@@ -106,6 +125,8 @@
                 pltpu.matmul_push_rhs(g_v[:, span], stage, 1, transpose=True)
                 pltpu.matmul_acc_lhs(in_mxu, pi_v[:, span], stage)
                 pltpu.matmul_acc_lhs(out_mxu, po_v[:, span], stage)
+            if c > CHUNKS - PIECES:
+                forward(c - (CHUNKS - PIECES + 1))
         return pltpu.matmul_pop(in_mxu), pltpu.matmul_pop(out_mxu)
 
     sums = (rank, rows)
@@ -138,17 +159,11 @@
             proj[unit][:, :2 * rank].astype(jnp.bfloat16).astype(jnp.float32)
         )
 
-    for i in range(1, n_chips):
-        for p in range(PIECES):
-            forward(i, p)
-
     own.wait()
     remote(queries, q_v.at[sibling], sib_send, sib_recv, (me_s, sibling)).wait_recv()
-    for i in range(1, n_chips):
-        for p in range(PIECES):
-            span = pl.ds(p * piece, piece)
-            there = q_v.at[lax.rem(chip - i + n_chips, n_chips) * 2 + 1 - core, :, span]
-            remote(there, there, fwd_send.at[i - 1, p], fwd_recv.at[i - 1, p], (me_s, sibling)).wait_recv()
+    for copy in far_in[(PIECES - 1) * (n_chips - 1):] + cross_in:
+        copy.wait_recv()
+
     n_q = q_v.shape[0] * q_v.shape[1]
     per = rows // n_q
     lines = n_ex * per
@@ -204,8 +219,8 @@
     total = recv_v[0]
     for s in range(1, n_sec):
         total += recv_v[s]
-    out[...] = total
-    for copy in far_out + [to_sibling] + fwd_out + sum_out:
+    out[...] = total * norm_factor
+    for copy in q_out + [to_sibling] + hand_on + sum_out:
         copy.wait_send()
 
 
@@ -229,8 +244,9 @@
         bf16, f32 = jnp.bfloat16, jnp.float32
         dma = pltpu.SemaphoreType.DMA
         hbm = pl.BlockSpec(memory_space=pl.ANY)
+        norm_factor = 1.0 / (rank * (slots * n_sec) ** 0.5)
         scores = pl.pallas_call(
-            functools.partial(kernel, n_sec, n_dp, n_ex),
+            functools.partial(kernel, n_sec, n_dp, n_ex, norm_factor),
             out_shape=jax.ShapeDtypeStruct((n_ex, n_dp * n_q), f32),
             in_specs=[hbm] * 6,
             out_specs=pl.BlockSpec(memory_space=pltpu.VMEM),
@@ -252,6 +268,8 @@
                 dma((n_far, PIECES)),
                 dma((n_far, PIECES)),
                 dma((n_far, PIECES)),
+                dma((n_far,)),
+                dma((n_far,)),
                 dma,
                 dma,
                 dma((n_sec - 1,)),
@@ -273,7 +291,6 @@
             queries[0],
             lengths,
         )
-        norm_factor = 1.0 / (rank * (slots * n_sec) ** 0.5)
-        return scores * norm_factor
+        return scores
 
     return jax.shard_map(body, mesh=mesh, in_specs=placed, out_specs=P("dp", None), check_vma=False)

time: 16.6 us -> 17 us (1.024)
  other arithmetic: 1.26 us -> 0 us
  local copies, waits for them, and re-layouts: 0 us -> 1.26 us
  Pallas kernels: 15.2 us -> 15.5 us
    mul x1 -> x0, other arithmetic: 1.26 us -> none  [body(): return scores * norm_factor]
    unnamed x0 -> x1, local copies, waits for them, and re-layouts: none -> 1.26 us
    pallas_call x1, Pallas kernels: 15.2 us -> 15.5 us  [body(): pl.pallas_call(functools.partial(kernel, n_sec, n_dp, n_ex, norm_factor),...]
where the time goes in v6:
time: 17 us; the launch traced here: 16.8 us
  Pallas kernels  15.5 us (91%)
  local copies, waits for them, and re-layouts  1.26 us (7%)
    pallas_call x1, Pallas kernels, body(): pl.pallas_call(functools.partial(kernel, n_sec, n_dp, n_ex, norm_factor),...  15.5 us
    unnamed x1, local copies, waits for them, and re-layouts  1.26 us

profile of v6, /device:TPU:0, one launch (start us, length us, event | category | flops | bytes accessed | tf_op | source)
XLA Modules:
  0.0 16.8 jit_solution(8980145890013501559)
XLA Ops:
  0.0 15.5 %shard_map.64 = f32[4,64]{1,0:T(4,128)} custom-call(bf16[256,8192]{1,0:T(8,128)(2,1)} %bitcast.5, bf16[256,8192]{1,0:T(8,128)(2,1)} %bitcast.6, bf16[64,8192]{1,0:T(8,128)(2,1)} %bitcast.7, bf16[64,8192]{1,0:T(8,128)(2,1)} %bitcast.8, bf16[16,4096]{1,0:T(8,128)(2,1)} %bitcast.9, s32[1,4]{1,0:T(1,128)} %lengths.1), custom_call_target="tpu_custom_call" | custom-call | flops 536870912 | bytes 10485760 | tf_op jit(solution)/shard_map/pallas_call | solution.py:248
  15.5 1.3 %copy.8 = f32[4,64]{1,0:T(4,128)} copy(f32[4,64]{1,0:T(4,128)} %shard_map.64) | data formatting | bytes 2048

commit v7 on v4

--- a/solution.py
+++ b/solution.py
@@ -8,8 +8,8 @@
 from jax.sharding import PartitionSpec as P
 
 MESH = pl.DeviceIdType.MESH
-CHUNKS = 8
-PIECES = 2
+CHUNKS = 4
+PIECES = 1
 NT = (((1,), (1,)), ((), ()))
 
 
@@ -46,14 +46,16 @@
         pl.semaphore_signal(barrier, inc=1, device_id=peer, device_id_type=MESH)
 
     loads = []
+    for k, (src, dst) in enumerate(((p_in, pi_v), (p_out, po_v))):
+        load = pltpu.make_async_copy(src, dst, load_sem.at[CHUNKS, k])
+        load.start()
+        loads.append(load)
     for c in range(CHUNKS):
         span = pl.ds(c * cols, cols)
-        four = []
-        for k, (src, dst) in enumerate(((p_in, pi_v), (acts, a_v), (p_out, po_v), (grads, g_v))):
+        for k, (src, dst) in enumerate(((acts, a_v), (grads, g_v))):
             load = pltpu.make_async_copy(src.at[:, span], dst.at[:, span], load_sem.at[c, k])
             load.start()
-            four.append(load)
-        loads.append(four)
+            loads.append(load)
     own = pltpu.make_async_copy(queries, q_v.at[me_d], own_sem)
     own.start()
     len_load = pltpu.make_async_copy(lengths, len_s, len_sem)
@@ -97,7 +99,7 @@
 
     def project(in_mxu, out_mxu):
         for c in range(CHUNKS):
-            for load in loads[c]:
+            for load in loads[2 * c + 2 if c else 0:2 * c + 4]:
                 load.wait()
             for t in range(cols // rows):
                 span = pl.ds(c * cols + t * rows, rows)
@@ -245,7 +247,7 @@
                 pltpu.VMEM((rows // 128, max(n_ex * rows // (n_dp * n_q), 16), 128), f32),
                 pltpu.VMEM((n_ex, n_dp * n_q), f32),
                 pltpu.VMEM((n_sec, n_ex, n_dp * n_q), f32),
-                dma((CHUNKS, 4)),
+                dma((CHUNKS + 1, 2)),
                 dma,
                 dma,
                 dma((n_far, PIECES)),

time: 16.6 us -> 16.5 us (level)
  Pallas kernels: 15.2 us -> 15 us
where the time goes in v7:
time: 16.5 us; the launch traced here: 16.3 us
  Pallas kernels  15 us (91%)
  other arithmetic  1.26 us (8%)
    pallas_call x1, Pallas kernels, body(): pl.pallas_call(functools.partial(kernel, n_sec, n_dp, n_ex), out_shape=ja...  15 us
    mul x1, other arithmetic, body(): return scores * norm_factor  1.26 us

profile of v7, /device:TPU:0, one launch (start us, length us, event | category | flops | bytes accessed | tf_op | source)
XLA Modules:
  0.0 16.3 jit_solution(7271832132591273709)
XLA Ops:
  0.0 15.0 %shard_map.64 = f32[4,64]{1,0:T(4,128)} custom-call(bf16[256,8192]{1,0:T(8,128)(2,1)} %bitcast.5, bf16[256,8192]{1,0:T(8,128)(2,1)} %bitcast.6, bf16[64,8192]{1,0:T(8,128)(2,1)} %bitcast.7, bf16[64,8192]{1,0:T(8,128)(2,1)} %bitcast.8, bf16[16,4096]{1,0:T(8,128)(2,1)} %bitcast.9, s32[1,4]{1,0:T(1,128)} %lengths.1), custom_call_target="tpu_custom_call" | custom-call | flops 536870912 | bytes 10485760 | tf_op jit(solution)/shard_map/pallas_call | solution.py:234
  15.0 1.3 %broadcast_multiply_fusion = f32[4,64]{1,0:T(4,128)} fusion(f32[4,64]{1,0:T(4,128)} %shard_map.64), kind=kLoop, calls=%fused_computation | loop fusion | flops 256 | bytes 2048 | tf_op jit(solution)/shard_map/mul | solution.py:279

commit v8 on v7

--- a/solution.py
+++ b/solution.py
@@ -16,7 +16,7 @@
 def kernel(
     n_sec, n_dp, n_ex,
     acts, grads, p_in, p_out, queries, lengths, out,
-    a_v, g_v, pi_v, po_v, q_v, len_s, rows_v, blocks_v, part_v, recv_v,
+    a_v, g_v, pi_v, po_v, q_v, len_s, rows_v, part_v, recv_v,
     load_sem, own_sem, len_sem, far_send, far_recv, fwd_send, fwd_recv,
     sib_send, sib_recv, sum_send, sum_recv,
 ):
@@ -82,20 +82,16 @@
     to_sibling = remote(queries, q_v.at[me_d], sib_send, sib_recv, (me_s, sibling))
     to_sibling.start()
 
-    fwd_out = []
-
-    def forward(i, p):
-        span = pl.ds(p * piece, piece)
-        here = q_v.at[chip_at(-i), :, span]
-        remote(
-            queries.at[:, span], here,
-            far_send.at[i - 1, p], far_recv.at[i - 1, p], (me_s, chip_at(i)),
-        ).wait_recv()
-        copy = remote(
-            here, here, fwd_send.at[i - 1, p], fwd_recv.at[i - 1, p], (me_s, sibling)
-        )
-        copy.start()
-        fwd_out.append(copy)
+    far_in, hand_on = [], []
+    for i in range(1, n_chips):
+        for p in range(PIECES):
+            here = q_v.at[chip_at(-i), :, pl.ds(p * piece, piece)]
+            far_in.append(remote(
+                here, here, far_send.at[i - 1, p], far_recv.at[i - 1, p], (me_s, chip_at(i))
+            ))
+            hand_on.append(remote(
+                here, here, fwd_send.at[i - 1, p], fwd_recv.at[i - 1, p], (me_s, sibling)
+            ))
 
     def project(in_mxu, out_mxu):
         for c in range(CHUNKS):
@@ -108,6 +104,9 @@
                 pltpu.matmul_push_rhs(g_v[:, span], stage, 1, transpose=True)
                 pltpu.matmul_acc_lhs(in_mxu, pi_v[:, span], stage)
                 pltpu.matmul_acc_lhs(out_mxu, po_v[:, span], stage)
+        for arrived, copy in zip(far_in, hand_on):
+            arrived.wait_recv()
+            copy.start()
         return pltpu.matmul_pop(in_mxu), pltpu.matmul_pop(out_mxu)
 
     sums = (rank, rows)
@@ -139,10 +138,6 @@
         rows_v[pl.ds(unit * half, half), :] = (
             proj[unit][:, :2 * rank].astype(jnp.bfloat16).astype(jnp.float32)
         )
-
-    for i in range(1, n_chips):
-        for p in range(PIECES):
-            forward(i, p)
 
     own.wait()
     remote(queries, q_v.at[sibling], sib_send, sib_recv, (me_s, sibling)).wait_recv()
@@ -180,14 +175,15 @@
     sums = (max(lines, 16), rows)
     blocks = pl.run_scoped(
         score, pltpu.ACC(0)(sums, jnp.float32), pltpu.ACC(1)(sums, jnp.float32)
-    )
-    lanes = blocks_v.shape[2]
-    for h in range(rows // lanes):
-        blocks_v[h] = blocks[:, h * lanes:(h + 1) * lanes]
-    part = jnp.zeros((n_ex, n_q), jnp.float32)
-    for b in range(per):
-        line = [blocks_v[h, pl.ds(b, n_ex, stride=per), :] for h in range(rows // lanes)]
-        part += jnp.concatenate(line, axis=1)[:, b * n_q:(b + 1) * n_q]
+    )[:lines]
+    line = lax.broadcasted_iota(jnp.int32, (lines, rows), 0)
+    column = lax.broadcasted_iota(jnp.int32, (lines, rows), 1)
+    own_block = lax.rem(line, per) == column // n_q
+    part = jnp.where(own_block, blocks, 0.0).reshape(n_ex, per, rows).sum(axis=1)
+    wide = rows
+    while wide > n_q:
+        wide //= 2
+        part = part[:, :wide] + part[:, wide:]
     part_v[...] = part
     recv_v[me_s] = part
 
@@ -207,7 +203,7 @@
     for s in range(1, n_sec):
         total += recv_v[s]
     out[...] = total
-    for copy in far_out + [to_sibling] + fwd_out + sum_out:
+    for copy in far_out + [to_sibling] + hand_on + sum_out:
         copy.wait_send()
 
 
@@ -244,7 +240,6 @@
                 pltpu.VMEM((n_dp, n_q, depth), bf16),
                 pltpu.SMEM(lengths.shape, jnp.int32),
                 pltpu.VMEM((n_ex * rank, 2 * rank), f32),
-                pltpu.VMEM((rows // 128, max(n_ex * rows // (n_dp * n_q), 16), 128), f32),
                 pltpu.VMEM((n_ex, n_dp * n_q), f32),
                 pltpu.VMEM((n_sec, n_ex, n_dp * n_q), f32),
                 dma((CHUNKS + 1, 2)),
@@ -260,7 +255,7 @@
                 dma((n_sec - 1,)),
             ],
             compiler_params=pltpu.CompilerParams(
-                collective_id=0, has_side_effects=True, vmem_limit_bytes=63 * 2**20
+                collective_id=0, has_side_effects=True, vmem_limit_bytes=54 * 2**20 - 80 * 2**10
             ),
             cost_estimate=pl.CostEstimate(
                 flops=4 * rows * width * rank,

time: 16.5 us -> 15.8 us (0.958)
  other arithmetic: 1.26 us -> 0.58 us
  local copies, waits for them, and re-layouts: 0 us -> 0.65 us
  Pallas kernels: 15 us -> 14.4 us
    mul x1, other arithmetic: 1.26 us -> 0.58 us  [body(): return scores * norm_factor]
    unnamed x0 -> x2, local copies, waits for them, and re-layouts: none -> 0.65 us
    pallas_call x1, Pallas kernels: 15 us -> 14.4 us  [body(): pl.pallas_call(functools.partial(kernel, n_sec, n_dp, n_ex), out_shape=ja...]
where the time goes in v8:
time: 15.8 us; the launch traced here: 15.7 us
  Pallas kernels  14.4 us (91%)
  local copies, waits for them, and re-layouts  0.65 us (4%)
  other arithmetic  0.58 us (4%)
    pallas_call x1, Pallas kernels, body(): pl.pallas_call(functools.partial(kernel, n_sec, n_dp, n_ex), out_shape=ja...  14.4 us
    unnamed x2, local copies, waits for them, and re-layouts  0.65 us
    mul x1, other arithmetic, body(): return scores * norm_factor  0.58 us

profile of v8, /device:TPU:0, one launch (start us, length us, event | category | flops | bytes accessed | tf_op | source)
XLA Modules:
  0.0 15.7 jit_solution(797499515403069274)
XLA Ops:
  0.0 0.0 copy-start
  0.0 0.7 %copy-done = s32[1,4]{1,0:T(1,128)S(1)} copy-done((s32[1,4]{1,0:T(1,128)S(1)}, s32[1,4]{1,0:T(1,128)}, u32[]{:S(2)}) %copy-start) | copy-done | bytes 40
  0.7 14.4 %shard_map.64 = f32[4,64]{1,0:T(4,128)S(1)} custom-call(bf16[256,8192]{1,0:T(8,128)(2,1)} %bitcast.5, bf16[256,8192]{1,0:T(8,128)(2,1)} %bitcast.6, bf16[64,8192]{1,0:T(8,128)(2,1)} %bitcast.7, bf16[64,8192]{1,0:T(8,128)(2,1)} %bitcast.8, bf16[16,4096]{1,0:T(8,128)(2,1)} %bitcast.9, s32[1,4]{1,0:T(1,128)S(1)} %copy-done), custom_call_target="tpu_custom_call" | custom-call | flops 536870912 | bytes 10485760 | tf_op jit(solution)/shard_map/pallas_call | solution.py:230
  15.1 0.6 %broadcast_multiply_fusion = f32[4,64]{1,0:T(4,128)} fusion(f32[4,64]{1,0:T(4,128)S(1)} %shard_map.64), kind=kLoop, calls=%fused_computation | loop fusion | flops 256 | bytes 2048 | tf_op jit(solution)/shard_map/mul | solution.py:274
Async XLA Ops:
  0.0 0.7 %copy-start = (s32[1,4]{1,0:T(1,128)S(1)}, s32[1,4]{1,0:T(1,128)}, u32[]{:S(2)}) copy-start(s32[1,4]{1,0:T(1,128)} %lengths.1) | copy-start | bytes 52

commit v9 on v8

--- a/solution.py
+++ b/solution.py
@@ -47,17 +47,14 @@
 
     loads = []
     for k, (src, dst) in enumerate(((p_in, pi_v), (p_out, po_v))):
-        load = pltpu.make_async_copy(src, dst, load_sem.at[CHUNKS, k])
-        load.start()
-        loads.append(load)
+        loads.append(pltpu.make_async_copy(src, dst, load_sem.at[CHUNKS, k]))
     for c in range(CHUNKS):
         span = pl.ds(c * cols, cols)
         for k, (src, dst) in enumerate(((acts, a_v), (grads, g_v))):
-            load = pltpu.make_async_copy(src.at[:, span], dst.at[:, span], load_sem.at[c, k])
-            load.start()
-            loads.append(load)
+            loads.append(pltpu.make_async_copy(src.at[:, span], dst.at[:, span], load_sem.at[c, k]))
+    for load in loads[:4]:
+        load.start()
     own = pltpu.make_async_copy(queries, q_v.at[me_d], own_sem)
-    own.start()
     len_load = pltpu.make_async_copy(lengths, len_s, len_sem)
     len_load.start()
 
@@ -81,6 +78,10 @@
             far_out.append(copy)
     to_sibling = remote(queries, q_v.at[me_d], sib_send, sib_recv, (me_s, sibling))
     to_sibling.start()
+
+    for load in loads[4:]:
+        load.start()
+    own.start()
 
     far_in, hand_on = [], []
     for i in range(1, n_chips):

time: 15.8 us -> 15.8 us (level)
  no operation moved by 1% of the time
where the time goes in v9:
time: 15.8 us; the launch traced here: 15.7 us
  Pallas kernels  14.4 us (91%)
  local copies, waits for them, and re-layouts  0.65 us (4%)
  other arithmetic  0.58 us (4%)
    pallas_call x1, Pallas kernels, body(): pl.pallas_call(functools.partial(kernel, n_sec, n_dp, n_ex), out_shape=ja...  14.4 us
    unnamed x2, local copies, waits for them, and re-layouts  0.65 us
    mul x1, other arithmetic, body(): return scores * norm_factor  0.58 us

profile of v9, /device:TPU:0, one launch (start us, length us, event | category | flops | bytes accessed | tf_op | source)
XLA Modules:
  0.0 15.7 jit_solution(10446808574364817678)
XLA Ops:
  0.0 0.0 copy-start
  0.0 0.7 %copy-done = s32[1,4]{1,0:T(1,128)S(1)} copy-done((s32[1,4]{1,0:T(1,128)S(1)}, s32[1,4]{1,0:T(1,128)}, u32[]{:S(2)}) %copy-start) | copy-done | bytes 40
  0.7 14.4 %shard_map.64 = f32[4,64]{1,0:T(4,128)S(1)} custom-call(bf16[256,8192]{1,0:T(8,128)(2,1)} %bitcast.5, bf16[256,8192]{1,0:T(8,128)(2,1)} %bitcast.6, bf16[64,8192]{1,0:T(8,128)(2,1)} %bitcast.7, bf16[64,8192]{1,0:T(8,128)(2,1)} %bitcast.8, bf16[16,4096]{1,0:T(8,128)(2,1)} %bitcast.9, s32[1,4]{1,0:T(1,128)S(1)} %copy-done), custom_call_target="tpu_custom_call" | custom-call | flops 536870912 | bytes 10485760 | tf_op jit(solution)/shard_map/pallas_call | solution.py:231
  15.1 0.6 %broadcast_multiply_fusion = f32[4,64]{1,0:T(4,128)} fusion(f32[4,64]{1,0:T(4,128)S(1)} %shard_map.64), kind=kLoop, calls=%fused_computation | loop fusion | flops 256 | bytes 2048 | tf_op jit(solution)/shard_map/mul | solution.py:275
Async XLA Ops:
  0.0 0.7 %copy-start = (s32[1,4]{1,0:T(1,128)S(1)}, s32[1,4]{1,0:T(1,128)}, u32[]{:S(2)}) copy-start(s32[1,4]{1,0:T(1,128)} %lengths.1) | copy-start | bytes 52

commit v10 on v9

--- a/solution.py
+++ b/solution.py
@@ -8,7 +8,7 @@
 from jax.sharding import PartitionSpec as P
 
 MESH = pl.DeviceIdType.MESH
-CHUNKS = 4
+CHUNKS = 8
 PIECES = 1
 NT = (((1,), (1,)), ((), ()))
 

time: 15.8 us -> 15.9 us (level)
  no operation moved by 1% of the time
where the time goes in v10:
time: 15.9 us; the launch traced here: 15.8 us
  Pallas kernels  14.5 us (91%)
  local copies, waits for them, and re-layouts  0.65 us (4%)
  other arithmetic  0.58 us (4%)
    pallas_call x1, Pallas kernels, body(): pl.pallas_call(functools.partial(kernel, n_sec, n_dp, n_ex), out_shape=ja...  14.5 us
    unnamed x2, local copies, waits for them, and re-layouts  0.65 us
    mul x1, other arithmetic, body(): return scores * norm_factor  0.58 us

profile of v10, /device:TPU:0, one launch (start us, length us, event | category | flops | bytes accessed | tf_op | source)
XLA Modules:
  0.0 15.8 jit_solution(5936389805274552245)
XLA Ops:
  0.0 0.0 copy-start
  0.0 0.7 %copy-done = s32[1,4]{1,0:T(1,128)S(1)} copy-done((s32[1,4]{1,0:T(1,128)S(1)}, s32[1,4]{1,0:T(1,128)}, u32[]{:S(2)}) %copy-start) | copy-done | bytes 40
  0.7 14.5 %shard_map.64 = f32[4,64]{1,0:T(4,128)S(1)} custom-call(bf16[256,8192]{1,0:T(8,128)(2,1)} %bitcast.5, bf16[256,8192]{1,0:T(8,128)(2,1)} %bitcast.6, bf16[64,8192]{1,0:T(8,128)(2,1)} %bitcast.7, bf16[64,8192]{1,0:T(8,128)(2,1)} %bitcast.8, bf16[16,4096]{1,0:T(8,128)(2,1)} %bitcast.9, s32[1,4]{1,0:T(1,128)S(1)} %copy-done), custom_call_target="tpu_custom_call" | custom-call | flops 536870912 | bytes 10485760 | tf_op jit(solution)/shard_map/pallas_call | solution.py:231
  15.2 0.6 %broadcast_multiply_fusion = f32[4,64]{1,0:T(4,128)} fusion(f32[4,64]{1,0:T(4,128)S(1)} %shard_map.64), kind=kLoop, calls=%fused_computation | loop fusion | flops 256 | bytes 2048 | tf_op jit(solution)/shard_map/mul | solution.py:275
Async XLA Ops:
  0.0 0.7 %copy-start = (s32[1,4]{1,0:T(1,128)S(1)}, s32[1,4]{1,0:T(1,128)}, u32[]{:S(2)}) copy-start(s32[1,4]{1,0:T(1,128)} %lengths.1) | copy-start | bytes 52
